TPU v7x, 128 devices: a whole 4x4x4 slice. The times are simulated.
128 devices in a mesh: freq: 16 (over x_hi, y, core), stn: 8 (over x_lo, z).
Axes of the slice: x: 4 (x_hi: 2, x_lo: 2; x = x_hi * 2 + x_lo), y: 4, z: 4, core: 2. Of those that a mesh axis runs over, the one named last changes fastest.
Arguments:
- voltages: bfloat16 [1024, 32, 4096], P('stn', 'freq'), may hold values from -6 to 6
- filter_taps: float32 [16, 4096], replicated, may hold values from -1.5 to 1.5
- station_flags: int32 [512, 32], replicated, may hold values from 0 to 1, as said below
Outputs:
- visibilities: float32 [256, 1024, 1024], P('freq', 'stn')
Inputs may be any that keep to these rules, and one draw needn't show every extreme that they name: `station_flags`: 1 keeps a station's data in that spectrum, 0 flags it.
All inputs are finite; a program needn't handle non-finite values.
Results may differ from a plain program's by a relative error of at most 0.0039.
Values may be sent and summed in bfloat16 or wider, within the bound.
No kernel may reach another device: no remote copies, remote signals or barrier semaphores. Data moves between devices by JAX's collectives and lax.ppermute only.
A program may use at most 192 MiB of HBM per device.

v0:
```python
import math
import jax
import jax.numpy as jnp
from jax import lax
from jax.sharding import PartitionSpec as P

AVG = 16


def from_behind(block, axis, distance):
    devices = range(lax.axis_size(axis))
    route = [(i - distance, i) for i in devices if i - distance in devices]
    return lax.ppermute(block, axis, route)


def dct_four(rows):
    highest = lax.Precision.HIGHEST
    count_rows, channels = rows.shape
    inner_len = 128
    outer_len = channels // inner_len
    positions = jnp.arange(channels).astype(jnp.float32)
    theta = math.pi * positions / (2 * channels)
    real_part = (rows * jnp.cos(theta)).reshape(count_rows, outer_len, inner_len)
    imag_part = (-rows * jnp.sin(theta)).reshape(count_rows, outer_len, inner_len)
    outer_idx = jnp.arange(outer_len, dtype=jnp.int32)
    outer_phase = (
        2
        * math.pi
        * (outer_idx[:, None] * outer_idx[None, :] % outer_len).astype(jnp.float32)
        / outer_len
    )
    outer_cos = jnp.cos(outer_phase)
    outer_sin = jnp.sin(outer_phase)
    section_real = jnp.einsum("pab,ak->pkb", real_part, outer_cos, precision=highest) + jnp.einsum(
        "pab,ak->pkb", imag_part, outer_sin, precision=highest
    )
    section_imag = jnp.einsum("pab,ak->pkb", imag_part, outer_cos, precision=highest) - jnp.einsum(
        "pab,ak->pkb", real_part, outer_sin, precision=highest
    )
    inner_idx = jnp.arange(inner_len, dtype=jnp.int32)
    twist_phase = (
        2 * math.pi * (outer_idx[:, None] * inner_idx[None, :]).astype(jnp.float32) / channels
    )
    twist_cos = jnp.cos(twist_phase)
    twist_sin = jnp.sin(twist_phase)
    twist_real = section_real * twist_cos + section_imag * twist_sin
    twist_imag = section_imag * twist_cos - section_real * twist_sin
    inner_phase = (
        2
        * math.pi
        * (inner_idx[:, None] * inner_idx[None, :] % inner_len).astype(jnp.float32)
        / inner_len
    )
    inner_cos = jnp.cos(inner_phase)
    inner_sin = jnp.sin(inner_phase)
    final_real = jnp.einsum("pkb,bq->pqk", twist_real, inner_cos, precision=highest) + jnp.einsum(
        "pkb,bq->pqk", twist_imag, inner_sin, precision=highest
    )
    final_imag = jnp.einsum("pkb,bq->pqk", twist_imag, inner_cos, precision=highest) - jnp.einsum(
        "pkb,bq->pqk", twist_real, inner_sin, precision=highest
    )
    final_real = final_real.reshape(count_rows, channels)
    final_imag = final_imag.reshape(count_rows, channels)
    post_angle = math.pi * (2 * positions + 1) / (4 * channels)
    return math.sqrt(2.0 / channels) * (
        final_real * jnp.cos(post_angle) + final_imag * jnp.sin(post_angle)
    )


def make_tile(mine, theirs):
    return jnp.einsum("gax,gbx->gab", mine, theirs, preferred_element_type=jnp.float32)


def body(voltages, filter_taps, station_flags):
    sig_dev, spec_dev, channels = voltages.shape
    tap_count = filter_taps.shape[0]
    history_len = tap_count - 1
    reach_count = -(-history_len // spec_dev)
    earlier = []
    for distance in range(1, reach_count + 1):
        needed = min(spec_dev, history_len - (distance - 1) * spec_dev)
        earlier.append(from_behind(voltages[:, spec_dev - needed :, :], "freq", distance))
    frames = jnp.concatenate(earlier[::-1] + [voltages], axis=1)
    window = jnp.zeros((sig_dev, spec_dev, channels), jnp.float32)
    for tap_index in range(tap_count):
        offset = history_len - tap_index
        window = window + filter_taps[tap_index][None, None, :] * frames[
            :, offset : offset + spec_dev, :
        ].astype(jnp.float32)
    channelized = dct_four(window.reshape(sig_dev * spec_dev, channels)).astype(jnp.bfloat16)
    groups_all = channels // AVG
    arranged = (
        channelized.reshape(sig_dev, spec_dev, groups_all, AVG)
        .transpose(2, 0, 1, 3)
        .reshape(groups_all, sig_dev, spec_dev * AVG)
    )
    turned = lax.all_to_all(arranged, "freq", split_axis=0, concat_axis=2, tiled=True)
    signal_flags = jnp.repeat(station_flags, 2, axis=0).astype(jnp.float32)
    position = lax.axis_index("stn")
    own_flags = lax.dynamic_slice_in_dim(signal_flags, position * sig_dev, sig_dev, 0)
    keep = jnp.repeat(own_flags, AVG, axis=1).astype(jnp.bfloat16)
    local = turned * keep[None]
    counts = jnp.dot(own_flags, signal_flags.T, precision=lax.Precision.HIGHEST)
    denominator = AVG * jnp.maximum(counts, 1.0)
    totals = make_tile(local, lax.all_gather(local, "stn", axis=1, tiled=True))
    return totals / denominator[None]


def solution(mesh):
    in_specs = (P("stn", "freq", None), P(), P())
    out_specs = P("freq", "stn", None)
    return jax.shard_map(body, mesh=mesh, in_specs=in_specs, out_specs=out_specs, check_vma=False)
```

profile of v0, /device:TPU:1, one launch (start us, length us, event | category | flops | bytes accessed | tf_op | source)
XLA Modules:
  0.0 907.7 jit_solution(544670661215522051)
XLA Ops:
  6.5 4.7 collective-permute-start
  11.3 3.3 collective-permute-start.1
  14.6 4.1 slice.106
  19.8 4.6 collective-permute-start.7
  24.5 5.2 collective-permute-start.2
  32.3 14.6 %collective-permute-done.7 = bf16[128,1,4096]{2,0,1:T(8,128)(2,1)S(1)} collective-permute-done((bf16[128,1,4096]{2,0,1:T(8,128)(2,1)S(1)}, bf16[128,1,4096]{2,0,1:T(8,128)(2,1)S(1)}, u32[]{:S(2)}, u32[]{:S(2)}) %collective-permute-start.7) | collective-permute-done | bytes 1048608 | tf_op jit(solution)/shard_map/ppermute | solution.py:13
  46.9 62.1 %collective-permute-start.4 = (bf16[128,2,4096]{2,1,0:T(2,128)(2,1)S(1)}, bf16[128,2,4096]{2,1,0:T(2,128)(2,1)}, u32[]{:S(2)}, u32[]{:S(2)}) collective-permute-start(bf16[128,2,4096]{2,1,0:T(2,128)(2,1)S(1)} %copy-done.2), channel_id=1, source_target_pairs={{0,40},{8,48},{16,56},{24,64},{32,72},{40,80},{48,88},{56,96},{64,... | collective-permute-start | bytes 6291464 | tf_op jit(solution)/shard_map/ppermute | solution.py:13
  109.0 65.9 %collective-permute-start.5 = (bf16[128,2,4096]{2,1,0:T(2,128)(2,1)S(1)}, bf16[128,2,4096]{2,1,0:T(2,128)(2,1)}, u32[]{:S(2)}, u32[]{:S(2)}) collective-permute-start(bf16[128,2,4096]{2,1,0:T(2,128)(2,1)S(1)} %copy-done.2), channel_id=1, source_target_pairs={{0,48},{8,56},{16,64},{24,72},{32,80},{40,88},{48,96},{56,104},{64... | collective-permute-start | bytes 6291464 | tf_op jit(solution)/shard_map/ppermute | solution.py:13
  176.3 2.8 collective-permute-start.6
  184.7 4.5 collective-permute-done.3
  189.2 51.1 %collective-permute-done.5 = bf16[128,2,4096]{2,1,0:T(2,128)(2,1)} collective-permute-done((bf16[128,2,4096]{2,1,0:T(2,128)(2,1)S(1)}, bf16[128,2,4096]{2,1,0:T(2,128)(2,1)}, u32[]{:S(2)}, u32[]{:S(2)}) %collective-permute-start.5) | collective-permute-done | bytes 2097184 | tf_op jit(solution)/shard_map/ppermute | solution.py:13
  240.3 61.7 %multiply_add_fusion = f32[128,2,4096]{2,1,0:T(2,128)} fusion(bf16[128,2,4096]{2,1,0:T(2,128)(2,1)} %collective-permute-done.6, bf16[128,2,4096]{2,1,0:T(2,128)(2,1)} %collective-permute-done.5, bf16[128,2,4096]{2,1,0:T(2,128)(2,1)} %collective-permute-done.4, bf16[128,2,4096]{2,1,0:T(2,128)(2,1)} %collective-permute-done.3, ...), kind=kLoop, calls=%fused_computation.8 | loop fusion | flops 74448896 | bytes 22282240 | tf_op jit(solution)/shard_map/add | solution.py:87
  302.0 6.6 reshape.108
  308.6 6.0 fusion.14
  314.6 4.1 fusion.9
  318.7 4.4 fusion.20
  323.1 5.1 add_bitcast_fusion.1
  328.3 6.0 fusion.3
  334.3 8.3 fusion.1
  342.5 8.0 add_bitcast_fusion
  350.5 14.5 %copy.49 = f32[256,128,32]{2,1,0:T(8,128)} copy(f32[256,128,32]{0,1,2:T(8,128)} %add_bitcast_fusion) | data formatting | bytes 8388608 | tf_op jit(solution)/shard_map/add | solution.py:56
  365.0 24.6 %reshape.109 = f32[128,2,256,16]{3,2,1,0:T(8,128)} reshape(f32[256,128,32]{2,1,0:T(8,128)} %copy.49) | data formatting | bytes 8388608 | tf_op jit(solution)/shard_map/reshape | solution.py:62
  389.7 11.4 %subtract_bitcast_fusion = f32[256,128,32]{0,1,2:T(8,128)} fusion(f32[128,256,32]{1,0,2:T(8,128)} %fusion.1, f32[256,32,128]{2,1,0:T(8,128)} %copy-done.1), kind=kOutput, calls=%fused_computation.3 | convolution fusion | flops 1611890688 | bytes 12582912 | tf_op jit(solution)/shard_map/pkb,bq->pqk/dot_general | solution.py:59
  401.1 14.5 %copy.53 = f32[256,128,32]{2,1,0:T(8,128)} copy(f32[256,128,32]{0,1,2:T(8,128)} %subtract_bitcast_fusion) | data formatting | bytes 8388608 | tf_op jit(solution)/shard_map/sub | solution.py:59
  415.7 24.4 %reshape.110 = f32[128,2,256,16]{3,2,1,0:T(8,128)} reshape(f32[256,128,32]{2,1,0:T(8,128)} %copy.53) | data formatting | bytes 8388608 | tf_op jit(solution)/shard_map/reshape | solution.py:63
  440.1 27.8 %fusion = bf16[256,128,2,16]{3,0,2,1:T(8,128)(2,1)} fusion(f32[128,2,256,16]{3,2,1,0:T(8,128)} %reshape.110, f32[128,2,256,16]{3,2,1,0:T(8,128)} %reshape.109, f32[256,16]{1,0:T(8,128)S(1)} %copy.54, f32[256,16]{1,0:T(8,128)S(1)} %copy.50), kind=kLoop, calls=%fused_computation.1 | loop fusion | flops 5242880 | bytes 10518528 | tf_op jit(solution)/shard_map/transpose | solution.py:94
  467.8 15.4 %copy.55 = bf16[256,128,2,16]{1,3,2,0:T(8,128)(2,1)} copy(bf16[256,128,2,16]{3,0,2,1:T(8,128)(2,1)} %fusion) | data formatting | bytes 4194304 | tf_op jit(solution)/shard_map/transpose | solution.py:94
  483.2 197.7 %all-to-all-start = ((bf16[256,128,32]{1,2,0:T(8,128)(2,1)}), bf16[256,128,32]{1,2,0:T(8,128)(2,1)S(1)}, u32[]{:S(2)}, u32[]{:S(2)}) async-start(bf16[256,128,32]{1,2,0:T(8,128)(2,1)} %bitcast.25), calls=%async_computation | async-start | bytes 4194304 | tf_op jit(solution)/shard_map/all_to_all | solution.py:97
  681.6 27.8 %all-to-all-done = bf16[256,128,32]{1,2,0:T(8,128)(2,1)S(1)} async-done(((bf16[256,128,32]{1,2,0:T(8,128)(2,1)}), bf16[256,128,32]{1,2,0:T(8,128)(2,1)S(1)}, u32[]{:S(2)}, u32[]{:S(2)}) %all-to-all-start) | async-done | bytes 2097184 | tf_op jit(solution)/shard_map/all_to_all | solution.py:97
  711.3 3.1 copy.60
  716.5 172.2 %all-gather.2.cloned.1.call-done = bf16[16,1024,512]{2,1,0:T(8,128)(2,1)} async-done(((bf16[16,128,512]{2,1,0:T(8,128)(2,1)}), bf16[16,1024,512]{2,1,0:T(8,128)(2,1)}) %all-gather.2.cloned.1.call-update) | async-done | bytes 16777232 | tf_op jit(solution)/shard_map/all_gather | solution.py:105
  888.7 11.7 %broadcast_divide_fusion = f32[16,128,1024]{2,1,0:T(8,128)} fusion(f32[128,1024]{1,0:T(8,128)S(1)} %fusion.27, bf16[16,128,512]{2,1,0:T(8,128)(2,1)} %broadcast_multiply_fusion, bf16[16,1024,512]{2,1,0:T(8,128)(2,1)} %all-gather.2.cloned.1.call-done), kind=kOutput, calls=%fused_computation.2 | convolution fusion | flops 2149580800 | bytes 27787264 | tf_op jit(solution)/shard_map/gax,gbx->gab/dot_general | solution.py:71
  (42 shorter events, 15.2 us)
Async XLA Ops:
  6.5 17.9 %copy-start.2 = (bf16[128,2,4096]{2,1,0:T(2,128)(2,1)S(1)}, bf16[128,2,4096]{2,1,0:T(2,128)(2,1)}, u32[]{:S(2)}) copy-start(bf16[128,2,4096]{2,1,0:T(2,128)(2,1)} %param.3) | copy-start | bytes 6291460
  6.5 102.5 %collective-permute-start = (bf16[128,2,4096]{2,1,0:T(2,128)(2,1)}, bf16[128,2,4096]{2,1,0:T(2,128)(2,1)S(1)}, u32[]{:S(2)}, u32[]{:S(2)}) collective-permute-start(bf16[128,2,4096]{2,1,0:T(2,128)(2,1)} %param.3), channel_id=1, source_target_pairs={{0,8},{8,16},{16,24},{24,32},{32,40},{40,48},{48,56},{56,64},{64,7... | collective-permute-start | bytes 6291464 | tf_op jit(solution)/shard_map/ppermute | solution.py:13
  11.3 163.7 %collective-permute-start.1 = (bf16[128,2,4096]{2,1,0:T(2,128)(2,1)}, bf16[128,2,4096]{2,1,0:T(2,128)(2,1)S(1)}, u32[]{:S(2)}, u32[]{:S(2)}) collective-permute-start(bf16[128,2,4096]{2,1,0:T(2,128)(2,1)} %param.3), channel_id=1, source_target_pairs={{0,16},{8,24},{16,32},{24,40},{32,48},{40,56},{48,64},{56,72},{64,... | collective-permute-start | bytes 6291464 | tf_op jit(solution)/shard_map/ppermute | solution.py:13
  19.8 27.1 %collective-permute-start.7 = (bf16[128,1,4096]{2,0,1:T(8,128)(2,1)S(1)}, bf16[128,1,4096]{2,0,1:T(8,128)(2,1)S(1)}, u32[]{:S(2)}, u32[]{:S(2)}) collective-permute-start(bf16[128,1,4096]{2,0,1:T(8,128)(2,1)S(1)} %copy.61), channel_id=1, source_target_pairs={{0,64},{8,72},{16,80},{24,88},{32,96},{40,104},{48,112},{56,120},{... | collective-permute-start | bytes 3145736 | tf_op jit(solution)/shard_map/ppermute | solution.py:13
  24.5 160.2 %collective-permute-start.2 = (bf16[128,2,4096]{2,1,0:T(2,128)(2,1)S(1)}, bf16[128,2,4096]{2,1,0:T(2,128)(2,1)}, u32[]{:S(2)}, u32[]{:S(2)}) collective-permute-start(bf16[128,2,4096]{2,1,0:T(2,128)(2,1)S(1)} %copy-done.2), channel_id=1, source_target_pairs={{0,24},{8,32},{16,40},{24,48},{32,56},{40,64},{48,72},{56,80},{64,... | collective-permute-start | bytes 6291464 | tf_op jit(solution)/shard_map/ppermute | solution.py:13
  29.7 159.5 %collective-permute-start.3 = (bf16[128,2,4096]{2,1,0:T(2,128)(2,1)S(1)}, bf16[128,2,4096]{2,1,0:T(2,128)(2,1)}, u32[]{:S(2)}, u32[]{:S(2)}) collective-permute-start(bf16[128,2,4096]{2,1,0:T(2,128)(2,1)S(1)} %copy-done.2), channel_id=1, source_target_pairs={{0,32},{8,40},{16,48},{24,56},{32,64},{40,72},{48,80},{56,88},{64,... | collective-permute-start | bytes 6291464 | tf_op jit(solution)/shard_map/ppermute | solution.py:13
  46.9 142.3 %collective-permute-start.4 = (bf16[128,2,4096]{2,1,0:T(2,128)(2,1)S(1)}, bf16[128,2,4096]{2,1,0:T(2,128)(2,1)}, u32[]{:S(2)}, u32[]{:S(2)}) collective-permute-start(bf16[128,2,4096]{2,1,0:T(2,128)(2,1)S(1)} %copy-done.2), channel_id=1, source_target_pairs={{0,40},{8,48},{16,56},{24,64},{32,72},{40,80},{48,88},{56,96},{64,... | collective-permute-start | bytes 6291464 | tf_op jit(solution)/shard_map/ppermute | solution.py:13
  109.0 65.9 %copy-start.3 = (bf16[128,2,4096]{2,1,0:T(2,128)(2,1)}, bf16[128,2,4096]{2,1,0:T(2,128)(2,1)S(1)}, u32[]{:S(2)}) copy-start(bf16[128,2,4096]{2,1,0:T(2,128)(2,1)S(1)} %collective-permute-done) | copy-start | bytes 6291460
  109.0 131.3 %collective-permute-start.5 = (bf16[128,2,4096]{2,1,0:T(2,128)(2,1)S(1)}, bf16[128,2,4096]{2,1,0:T(2,128)(2,1)}, u32[]{:S(2)}, u32[]{:S(2)}) collective-permute-start(bf16[128,2,4096]{2,1,0:T(2,128)(2,1)S(1)} %copy-done.2), channel_id=1, source_target_pairs={{0,48},{8,56},{16,64},{24,72},{32,80},{40,88},{48,96},{56,104},{64... | collective-permute-start | bytes 6291464 | tf_op jit(solution)/shard_map/ppermute | solution.py:13
  174.9 1.3 copy-start.5
  176.3 64.1 %collective-permute-start.6 = (bf16[128,2,4096]{2,1,0:T(2,128)(2,1)S(1)}, bf16[128,2,4096]{2,1,0:T(2,128)(2,1)}, u32[]{:S(2)}, u32[]{:S(2)}) collective-permute-start(bf16[128,2,4096]{2,1,0:T(2,128)(2,1)S(1)} %copy-done.2), channel_id=1, source_target_pairs={{0,56},{8,64},{16,72},{24,80},{32,88},{40,96},{48,104},{56,112},{6... | collective-permute-start | bytes 6291464 | tf_op jit(solution)/shard_map/ppermute | solution.py:13
  179.4 60.9 %copy-start.4 = (bf16[128,2,4096]{2,1,0:T(2,128)(2,1)S(1)}, bf16[128,2,4096]{2,1,0:T(2,128)(2,1)}, u32[]{:S(2)}) copy-start(bf16[128,2,4096]{2,1,0:T(2,128)(2,1)} %copy-done.3) | copy-start | bytes 6291460
  308.6 6.0 copy-start
  328.2 14.3 %copy-start.1 = (f32[256,32,128]{2,1,0:T(8,128)}, f32[256,32,128]{2,1,0:T(8,128)S(1)}, u32[]{:S(2)}) copy-start(f32[256,32,128]{2,1,0:T(8,128)S(1)} %get-tuple-element.5) | copy-start | bytes 12582916
  483.2 197.7 %copy-start.6 = (s32[512,32]{0,1:T(8,128)S(1)}, s32[512,32]{0,1:T(8,128)}, u32[]{:S(2)}) copy-start(s32[512,32]{0,1:T(8,128)} %param.5) | copy-start | bytes 196612
  483.2 226.2 %all-to-all-start = ((bf16[256,128,32]{1,2,0:T(8,128)(2,1)}), bf16[256,128,32]{1,2,0:T(8,128)(2,1)S(1)}, u32[]{:S(2)}, u32[]{:S(2)}) async-start(bf16[256,128,32]{1,2,0:T(8,128)(2,1)} %bitcast.25), calls=%async_computation | async-start | bytes 4194304 | tf_op jit(solution)/shard_map/all_to_all | solution.py:97
  680.9 207.8 %all-gather.2.cloned.1.call-start = ((), (), s32[]{:S(2)}) async-start(), calls=%async_computation.1 | async-start | bytes 18874368 | tf_op jit(solution)/shard_map/all_gather | solution.py:105
Sparse Core Ops, SparseCore 0:
  716.0 172.6 all-gather.1
where the time goes:
time: 914 us; the launch traced here: 908 us
  starting transfers between devices  349 us (38%)
  waiting for transfers between devices  270 us (30%)
  local copies, waits for them, and re-layouts  117 us (13%)
  other arithmetic  91.3 us (10%)
  matrix products  65.6 us (7%)
  between operations  14.2 us (2%)
    all_to_all x1, starting transfers between devices, body(): lax.all_to_all(arranged, 'freq', split_axis=0, concat_axis=2, tiled=True)  198 us
    all_gather x1, waiting for transfers between devices, body(): totals = make_tile(local, lax.all_gather(local, 'stn', axis=1, tiled=True))  172 us
    ppermute x8, starting transfers between devices, from_behind(): return lax.ppermute(block, axis, route)  151 us
    ppermute x8, waiting for transfers between devices, from_behind(): return lax.ppermute(block, axis, route)  70.3 us
    add x1, other arithmetic, body(): window + filter_taps[tap_index][None, None, :] * frames[:, offset:offset...  61.7 us
    all_to_all x1, waiting for transfers between devices, body(): lax.all_to_all(arranged, 'freq', split_axis=0, concat_axis=2, tiled=True)  27.8 us
    transpose x1, other arithmetic, body(): arranged = channelized.reshape(sig_dev, spec_dev, groups_all, AVG).transp...  27.8 us
    reshape x1, local copies, waits for them, and re-layouts, dct_four(): final_real = final_real.reshape(count_rows, channels)  24.6 us
  transfers between devices with their start and end apart: 10, of which 5 were waited for; matrix products, arithmetic and copies ran while one was open for 1% of the time, Pallas kernels for 0%

commit v1 on v0

--- a/solution.py
+++ b/solution.py
@@ -94,7 +94,10 @@
         .transpose(2, 0, 1, 3)
         .reshape(groups_all, sig_dev, spec_dev * AVG)
     )
-    turned = lax.all_to_all(arranged, "freq", split_axis=0, concat_axis=2, tiled=True)
+    size = lax.axis_size("freq")
+    shards = jnp.stack(jnp.split(arranged, size, axis=0), axis=0)
+    shards = lax.all_to_all(shards, "freq", split_axis=0, concat_axis=0)
+    turned = jnp.concatenate(shards, axis=2)
     signal_flags = jnp.repeat(station_flags, 2, axis=0).astype(jnp.float32)
     position = lax.axis_index("stn")
     own_flags = lax.dynamic_slice_in_dim(signal_flags, position * sig_dev, sig_dev, 0)

time: 914 us -> 965 us (1.056)
  local copies, waits for them, and re-layouts: 117 us -> 168 us
    split x0 -> x17, local copies, waits for them, and re-layouts: none -> 49.6 us  [body(): shards = jnp.stack(jnp.split(arranged, size, axis=0), axis=0)]
    unnamed x17 -> x38, local copies, waits for them, and re-layouts: 2.57 us -> 18.9 us
    transpose x1 -> x0, local copies, waits for them, and re-layouts: 15.4 us -> none  [body(): arranged = channelized.reshape(sig_dev, spec_dev, groups_all, AVG).transp...]
where the time goes in v1:
time: 965 us; the launch traced here: 958 us
  starting transfers between devices  349 us (36%)
  waiting for transfers between devices  270 us (28%)
  local copies, waits for them, and re-layouts  168 us (17%)
  other arithmetic  91.2 us (9%)
  matrix products  65.5 us (7%)
  between operations  14 us (1%)
    all_to_all x1, starting transfers between devices, body(): shards = lax.all_to_all(shards, 'freq', split_axis=0, concat_axis=0)  198 us
    all_gather x1, waiting for transfers between devices, body(): totals = make_tile(local, lax.all_gather(local, 'stn', axis=1, tiled=True))  172 us
    ppermute x8, starting transfers between devices, from_behind(): return lax.ppermute(block, axis, route)  152 us
    ppermute x8, waiting for transfers between devices, from_behind(): return lax.ppermute(block, axis, route)  70.1 us
    add x1, other arithmetic, body(): window + filter_taps[tap_index][None, None, :] * frames[:, offset:offset...  61.6 us
    split x17, local copies, waits for them, and re-layouts, body(): shards = jnp.stack(jnp.split(arranged, size, axis=0), axis=0)  49.6 us
    all_to_all x1, waiting for transfers between devices, body(): shards = lax.all_to_all(shards, 'freq', split_axis=0, concat_axis=0)  27.8 us
    transpose x1, other arithmetic, body(): arranged = channelized.reshape(sig_dev, spec_dev, groups_all, AVG).transp...  27.7 us
  transfers between devices with their start and end apart: 10, of which 5 were waited for; matrix products, arithmetic and copies ran while one was open for 1% of the time, Pallas kernels for 0%

profile of v1, /device:TPU:1, one launch (start us, length us, event | category | flops | bytes accessed | tf_op | source)
XLA Modules:
  0.0 958.1 jit_solution(7138966283315117398)
XLA Ops:
  6.5 4.7 collective-permute-start
  11.3 3.3 collective-permute-start.1
  14.6 4.1 slice.122
  19.8 4.6 collective-permute-start.7
  24.5 5.2 collective-permute-start.2
  32.4 14.6 %collective-permute-done.7 = bf16[128,1,4096]{2,0,1:T(8,128)(2,1)S(1)} collective-permute-done((bf16[128,1,4096]{2,0,1:T(8,128)(2,1)S(1)}, bf16[128,1,4096]{2,0,1:T(8,128)(2,1)S(1)}, u32[]{:S(2)}, u32[]{:S(2)}) %collective-permute-start.7) | collective-permute-done | bytes 1048608 | tf_op jit(solution)/shard_map/ppermute | solution.py:13
  46.9 62.1 %collective-permute-start.4 = (bf16[128,2,4096]{2,1,0:T(2,128)(2,1)S(1)}, bf16[128,2,4096]{2,1,0:T(2,128)(2,1)}, u32[]{:S(2)}, u32[]{:S(2)}) collective-permute-start(bf16[128,2,4096]{2,1,0:T(2,128)(2,1)S(1)} %copy-done.2), channel_id=1, source_target_pairs={{0,40},{8,48},{16,56},{24,64},{32,72},{40,80},{48,88},{56,96},{64,... | collective-permute-start | bytes 6291464 | tf_op jit(solution)/shard_map/ppermute | solution.py:13
  109.0 65.9 %collective-permute-start.5 = (bf16[128,2,4096]{2,1,0:T(2,128)(2,1)S(1)}, bf16[128,2,4096]{2,1,0:T(2,128)(2,1)}, u32[]{:S(2)}, u32[]{:S(2)}) collective-permute-start(bf16[128,2,4096]{2,1,0:T(2,128)(2,1)S(1)} %copy-done.2), channel_id=1, source_target_pairs={{0,48},{8,56},{16,64},{24,72},{32,80},{40,88},{48,96},{56,104},{64... | collective-permute-start | bytes 6291464 | tf_op jit(solution)/shard_map/ppermute | solution.py:13
  176.3 3.1 collective-permute-start.6
  184.8 4.4 collective-permute-done.3
  189.2 51.1 %collective-permute-done.5 = bf16[128,2,4096]{2,1,0:T(2,128)(2,1)} collective-permute-done((bf16[128,2,4096]{2,1,0:T(2,128)(2,1)S(1)}, bf16[128,2,4096]{2,1,0:T(2,128)(2,1)}, u32[]{:S(2)}, u32[]{:S(2)}) %collective-permute-start.5) | collective-permute-done | bytes 2097184 | tf_op jit(solution)/shard_map/ppermute | solution.py:13
  240.3 61.6 %multiply_add_fusion = f32[128,2,4096]{2,1,0:T(2,128)} fusion(bf16[128,2,4096]{2,1,0:T(2,128)(2,1)} %collective-permute-done.6, bf16[128,2,4096]{2,1,0:T(2,128)(2,1)} %collective-permute-done.5, bf16[128,2,4096]{2,1,0:T(2,128)(2,1)} %collective-permute-done.4, bf16[128,2,4096]{2,1,0:T(2,128)(2,1)} %collective-permute-done.3, ...), kind=kLoop, calls=%fused_computation.8 | loop fusion | flops 74448896 | bytes 22282240 | tf_op jit(solution)/shard_map/add | solution.py:87
  301.9 6.6 reshape.144
  308.5 5.7 fusion.14
  314.3 4.1 fusion.9
  318.3 4.4 fusion.20
  322.8 5.1 add_bitcast_fusion.1
  327.9 6.0 fusion.3
  333.9 8.5 fusion.1
  342.4 8.0 add_bitcast_fusion
  350.3 14.5 %copy.94 = f32[256,128,32]{2,1,0:T(8,128)} copy(f32[256,128,32]{0,1,2:T(8,128)} %add_bitcast_fusion) | data formatting | bytes 8388608 | tf_op jit(solution)/shard_map/add | solution.py:56
  364.9 24.6 %reshape.145 = f32[128,2,256,16]{3,2,1,0:T(8,128)} reshape(f32[256,128,32]{2,1,0:T(8,128)} %copy.94) | data formatting | bytes 8388608 | tf_op jit(solution)/shard_map/reshape | solution.py:62
  389.5 11.4 %subtract_bitcast_fusion = f32[256,128,32]{0,1,2:T(8,128)} fusion(f32[128,256,32]{1,0,2:T(8,128)} %fusion.1, f32[256,32,128]{2,1,0:T(8,128)} %copy-done.1), kind=kOutput, calls=%fused_computation.3 | convolution fusion | flops 1611890688 | bytes 12582912 | tf_op jit(solution)/shard_map/pkb,bq->pqk/dot_general | solution.py:59
  400.9 14.5 %copy.98 = f32[256,128,32]{2,1,0:T(8,128)} copy(f32[256,128,32]{0,1,2:T(8,128)} %subtract_bitcast_fusion) | data formatting | bytes 8388608 | tf_op jit(solution)/shard_map/sub | solution.py:59
  415.4 24.4 %reshape.146 = f32[128,2,256,16]{3,2,1,0:T(8,128)} reshape(f32[256,128,32]{2,1,0:T(8,128)} %copy.98) | data formatting | bytes 8388608 | tf_op jit(solution)/shard_map/reshape | solution.py:63
  439.9 27.7 %fusion = bf16[256,128,2,16]{3,0,2,1:T(8,128)(2,1)} fusion(f32[128,2,256,16]{3,2,1,0:T(8,128)} %reshape.146, f32[128,2,256,16]{3,2,1,0:T(8,128)} %reshape.145, f32[256,16]{1,0:T(8,128)S(1)} %copy.99, f32[256,16]{1,0:T(8,128)S(1)} %copy.95), kind=kLoop, calls=%fused_computation.1 | loop fusion | flops 5242880 | bytes 10518528 | tf_op jit(solution)/shard_map/transpose | solution.py:94
  467.6 11.7 %fusion.98 = (bf16[16,128,2,16]{3,0,2,1:T(8,128)(2,1)S(1)}, bf16[16,128,2,16]{3,0,2,1:T(8,128)(2,1)S(1)}, bf16[16,128,2,16]{3,0,2,1:T(8,128)(2,1)S(1)}, bf16[16,...) fusion(bf16[256,128,2,16]{3,0,2,1:T(8,128)(2,1)} %fusion), kind=kLoop, calls=%fused_computation.128 | loop fusion | bytes 4194304 | tf_op jit(solution)/shard_map/split | solution.py:98
  534.2 197.6 %all-to-all-start = ((bf16[16,16,128,32]{2,3,1,0:T(8,128)(2,1)}), bf16[16,16,128,32]{2,3,1,0:T(8,128)(2,1)S(1)}, u32[]{:S(2)}, u32[]{:S(2)}) async-start(bf16[16,16,128,32]{2,3,1,0:T(8,128)(2,1)} %constant_dynamic-update-slice_fusion), calls=%async_computation | async-start | bytes 4194304 | tf_op jit(solution)/shard_map/all_to_all | solution.py:99
  732.5 27.8 %all-to-all-done = bf16[16,16,128,32]{2,3,1,0:T(8,128)(2,1)S(1)} async-done(((bf16[16,16,128,32]{2,3,1,0:T(8,128)(2,1)}), bf16[16,16,128,32]{2,3,1,0:T(8,128)(2,1)S(1)}, u32[]{:S(2)}, u32[]{:S(2)}) %all-to-all-start) | async-done | bytes 2097184 | tf_op jit(solution)/shard_map/all_to_all | solution.py:99
  762.2 2.9 copy.120
  767.1 172.2 %all-gather.2.cloned.1.call-done = bf16[16,1024,512]{2,1,0:T(8,128)(2,1)} async-done(((bf16[16,128,512]{2,1,0:T(8,128)(2,1)}), bf16[16,1024,512]{2,1,0:T(8,128)(2,1)}) %all-gather.2.cloned.1.call-update) | async-done | bytes 16777232 | tf_op jit(solution)/shard_map/all_gather | solution.py:108
  939.3 11.7 %broadcast_divide_fusion = f32[16,128,1024]{2,1,0:T(8,128)} fusion(f32[128,1024]{1,0:T(8,128)S(1)} %fusion.27, bf16[16,128,512]{2,1,0:T(8,128)(2,1)} %broadcast_multiply_fusion, bf16[16,1024,512]{2,1,0:T(8,128)(2,1)} %all-gather.2.cloned.1.call-done), kind=kOutput, calls=%fused_computation.2 | convolution fusion | flops 2149580800 | bytes 27787264 | tf_op jit(solution)/shard_map/gax,gbx->gab/dot_general | solution.py:71
  (80 shorter events, 70.0 us)
Async XLA Ops:
  6.5 17.9 %copy-start.2 = (bf16[128,2,4096]{2,1,0:T(2,128)(2,1)S(1)}, bf16[128,2,4096]{2,1,0:T(2,128)(2,1)}, u32[]{:S(2)}) copy-start(bf16[128,2,4096]{2,1,0:T(2,128)(2,1)} %param.3) | copy-start | bytes 6291460
  6.5 102.5 %collective-permute-start = (bf16[128,2,4096]{2,1,0:T(2,128)(2,1)}, bf16[128,2,4096]{2,1,0:T(2,128)(2,1)S(1)}, u32[]{:S(2)}, u32[]{:S(2)}) collective-permute-start(bf16[128,2,4096]{2,1,0:T(2,128)(2,1)} %param.3), channel_id=1, source_target_pairs={{0,8},{8,16},{16,24},{24,32},{32,40},{40,48},{48,56},{56,64},{64,7... | collective-permute-start | bytes 6291464 | tf_op jit(solution)/shard_map/ppermute | solution.py:13
  11.3 163.7 %collective-permute-start.1 = (bf16[128,2,4096]{2,1,0:T(2,128)(2,1)}, bf16[128,2,4096]{2,1,0:T(2,128)(2,1)S(1)}, u32[]{:S(2)}, u32[]{:S(2)}) collective-permute-start(bf16[128,2,4096]{2,1,0:T(2,128)(2,1)} %param.3), channel_id=1, source_target_pairs={{0,16},{8,24},{16,32},{24,40},{32,48},{40,56},{48,64},{56,72},{64,... | collective-permute-start | bytes 6291464 | tf_op jit(solution)/shard_map/ppermute | solution.py:13
  19.8 27.1 %collective-permute-start.7 = (bf16[128,1,4096]{2,0,1:T(8,128)(2,1)S(1)}, bf16[128,1,4096]{2,0,1:T(8,128)(2,1)S(1)}, u32[]{:S(2)}, u32[]{:S(2)}) collective-permute-start(bf16[128,1,4096]{2,0,1:T(8,128)(2,1)S(1)} %copy.121), channel_id=1, source_target_pairs={{0,64},{8,72},{16,80},{24,88},{32,96},{40,104},{48,112},{56,120},{... | collective-permute-start | bytes 3145736 | tf_op jit(solution)/shard_map/ppermute | solution.py:13
  24.5 160.3 %collective-permute-start.2 = (bf16[128,2,4096]{2,1,0:T(2,128)(2,1)S(1)}, bf16[128,2,4096]{2,1,0:T(2,128)(2,1)}, u32[]{:S(2)}, u32[]{:S(2)}) collective-permute-start(bf16[128,2,4096]{2,1,0:T(2,128)(2,1)S(1)} %copy-done.2), channel_id=1, source_target_pairs={{0,24},{8,32},{16,40},{24,48},{32,56},{40,64},{48,72},{56,80},{64,... | collective-permute-start | bytes 6291464 | tf_op jit(solution)/shard_map/ppermute | solution.py:13
  29.7 159.5 %collective-permute-start.3 = (bf16[128,2,4096]{2,1,0:T(2,128)(2,1)S(1)}, bf16[128,2,4096]{2,1,0:T(2,128)(2,1)}, u32[]{:S(2)}, u32[]{:S(2)}) collective-permute-start(bf16[128,2,4096]{2,1,0:T(2,128)(2,1)S(1)} %copy-done.2), channel_id=1, source_target_pairs={{0,32},{8,40},{16,48},{24,56},{32,64},{40,72},{48,80},{56,88},{64,... | collective-permute-start | bytes 6291464 | tf_op jit(solution)/shard_map/ppermute | solution.py:13
  46.9 142.3 %collective-permute-start.4 = (bf16[128,2,4096]{2,1,0:T(2,128)(2,1)S(1)}, bf16[128,2,4096]{2,1,0:T(2,128)(2,1)}, u32[]{:S(2)}, u32[]{:S(2)}) collective-permute-start(bf16[128,2,4096]{2,1,0:T(2,128)(2,1)S(1)} %copy-done.2), channel_id=1, source_target_pairs={{0,40},{8,48},{16,56},{24,64},{32,72},{40,80},{48,88},{56,96},{64,... | collective-permute-start | bytes 6291464 | tf_op jit(solution)/shard_map/ppermute | solution.py:13
  109.0 65.9 %copy-start.3 = (bf16[128,2,4096]{2,1,0:T(2,128)(2,1)}, bf16[128,2,4096]{2,1,0:T(2,128)(2,1)S(1)}, u32[]{:S(2)}) copy-start(bf16[128,2,4096]{2,1,0:T(2,128)(2,1)S(1)} %collective-permute-done) | copy-start | bytes 6291460
  109.0 131.3 %collective-permute-start.5 = (bf16[128,2,4096]{2,1,0:T(2,128)(2,1)S(1)}, bf16[128,2,4096]{2,1,0:T(2,128)(2,1)}, u32[]{:S(2)}, u32[]{:S(2)}) collective-permute-start(bf16[128,2,4096]{2,1,0:T(2,128)(2,1)S(1)} %copy-done.2), channel_id=1, source_target_pairs={{0,48},{8,56},{16,64},{24,72},{32,80},{40,88},{48,96},{56,104},{64... | collective-permute-start | bytes 6291464 | tf_op jit(solution)/shard_map/ppermute | solution.py:13
  174.9 1.3 copy-start.5
  176.3 64.1 %collective-permute-start.6 = (bf16[128,2,4096]{2,1,0:T(2,128)(2,1)S(1)}, bf16[128,2,4096]{2,1,0:T(2,128)(2,1)}, u32[]{:S(2)}, u32[]{:S(2)}) collective-permute-start(bf16[128,2,4096]{2,1,0:T(2,128)(2,1)S(1)} %copy-done.2), channel_id=1, source_target_pairs={{0,56},{8,64},{16,72},{24,80},{32,88},{40,96},{48,104},{56,112},{6... | collective-permute-start | bytes 6291464 | tf_op jit(solution)/shard_map/ppermute | solution.py:13
  179.8 60.6 %copy-start.4 = (bf16[128,2,4096]{2,1,0:T(2,128)(2,1)S(1)}, bf16[128,2,4096]{2,1,0:T(2,128)(2,1)}, u32[]{:S(2)}) copy-start(bf16[128,2,4096]{2,1,0:T(2,128)(2,1)} %copy-done.3) | copy-start | bytes 6291460
  308.5 5.8 copy-start
  327.9 14.5 %copy-start.1 = (f32[256,32,128]{2,1,0:T(8,128)}, f32[256,32,128]{2,1,0:T(8,128)S(1)}, u32[]{:S(2)}) copy-start(f32[256,32,128]{2,1,0:T(8,128)S(1)} %get-tuple-element.21) | copy-start | bytes 12582916
  515.8 13.1 %copy-start.8 = (bf16[16,128,2,16]{1,3,2,0:T(8,128)(2,1)S(1)}, bf16[16,128,2,16]{1,3,2,0:T(8,128)(2,1)}, u32[]{:S(2)}) copy-start(bf16[16,128,2,16]{1,3,2,0:T(8,128)(2,1)} %copy.108) | copy-start | bytes 393220
  515.8 13.8 %copy-start.7 = (bf16[16,128,2,16]{1,3,2,0:T(8,128)(2,1)S(1)}, bf16[16,128,2,16]{1,3,2,0:T(8,128)(2,1)}, u32[]{:S(2)}) copy-start(bf16[16,128,2,16]{1,3,2,0:T(8,128)(2,1)} %copy.109) | copy-start | bytes 393220
  515.8 14.4 %copy-start.6 = (bf16[16,128,2,16]{1,3,2,0:T(8,128)(2,1)S(1)}, bf16[16,128,2,16]{1,3,2,0:T(8,128)(2,1)}, u32[]{:S(2)}) copy-start(bf16[16,128,2,16]{1,3,2,0:T(8,128)(2,1)} %copy.110) | copy-start | bytes 393220
  517.9 213.9 %copy-start.9 = (s32[512,32]{0,1:T(8,128)S(1)}, s32[512,32]{0,1:T(8,128)}, u32[]{:S(2)}) copy-start(s32[512,32]{0,1:T(8,128)} %param.5) | copy-start | bytes 196612
  534.2 226.0 %all-to-all-start = ((bf16[16,16,128,32]{2,3,1,0:T(8,128)(2,1)}), bf16[16,16,128,32]{2,3,1,0:T(8,128)(2,1)S(1)}, u32[]{:S(2)}, u32[]{:S(2)}) async-start(bf16[16,16,128,32]{2,3,1,0:T(8,128)(2,1)} %constant_dynamic-update-slice_fusion), calls=%async_computation | async-start | bytes 4194304 | tf_op jit(solution)/shard_map/all_to_all | solution.py:99
  731.8 207.5 %all-gather.2.cloned.1.call-start = ((), (), s32[]{:S(2)}) async-start(), calls=%async_computation.1 | async-start | bytes 18874368 | tf_op jit(solution)/shard_map/all_gather | solution.py:108
Sparse Core Ops, SparseCore 0:
  766.7 172.6 all-gather.1
